TPU v7x, 32 devices: a whole 2x2x4 slice. The times are simulated.
32 devices in a mesh: parts: 2 (over y), ctx: 4 (over z), wt: 2 (over x), sub: 2 (over core).
Axes of the slice: x: 2, y: 2, z: 4, core: 2. Of those that a mesh axis runs over, the one named last changes fastest.
Arguments:
- tokens: bfloat16 [2048, 4096], P(('parts', 'ctx', 'wt')), parts along dimension 0, may hold values from -6 to 6
- block_order: int32 [32], P('parts'), parts along dimension 0, may hold values from 0 to 15, each once
- q_weight: bfloat16 [4096, 2048], P('wt', 'sub')
- key_value_weight: bfloat16 [4096, 4, 2, 128], P('wt', 'sub'), may hold values from -0.09375 to 0.09375
- out_weight: bfloat16 [2048, 4096], P('sub', 'wt'), may hold values from -0.5 to 0.5
Outputs:
- attended: bfloat16 [2048, 4096], P(('parts', 'ctx', 'wt'), 'sub'), parts along dimension 0
There are 2 independent parts, one for each index of `parts`. A program takes and returns all parts, laid end to end along the dimension named above; an argument that names none is the same for every part. Nothing has to cross between parts.
Inputs may be any that keep to these rules, and one draw needn't show every extreme that they name: block_order is a permutation of the 16 block numbers.
All inputs are finite; a program needn't handle non-finite values.
Results may differ from a plain program's by a relative error of at most 0.014.
The roundings to bfloat16 on the way count: a program that leaves them out, or rounds other values in their place, can miss the bound.
Values may be sent and summed in bfloat16 or wider, within the bound.
A program may use at most 128 MiB of HBM per device.

v0:
```python
import jax
import jax.numpy as jnp
from jax import lax
from jax.sharding import PartitionSpec as P

rope_base = 500000.0
epsilon = 1e-05


def token_positions(row_ids, block_order, block_len):
    number = block_order.shape[0]
    blocks = row_ids // block_len
    equal = blocks[:, None] == jnp.arange(number, dtype=jnp.int32)[None, :]
    chosen = jnp.sum(jnp.where(equal, block_order[None, :], 0), axis=1)
    return chosen * block_len + row_ids % block_len


def rotary(values_in, positions, head_dim):
    half_dim = head_dim // 2
    inverse_freq = rope_base ** (-(jnp.arange(half_dim, dtype=jnp.float32) * 2.0 / head_dim))
    angles = positions.astype(jnp.float32)[:, None] * inverse_freq[None, :]
    cosine = jnp.concatenate([jnp.cos(angles), jnp.cos(angles)], axis=1)[:, None, :]
    sine = jnp.concatenate([jnp.sin(angles), jnp.sin(angles)], axis=1)[:, None, :]
    rotated = jnp.concatenate([-values_in[..., half_dim:], values_in[..., :half_dim]], axis=-1)
    return values_in * cosine + rotated * sine


def body(tokens, block_order, q_weight, key_value_weight, out_weight):
    tok_rows = tokens.shape[0]
    block_len = tok_rows // 2
    head_dim = key_value_weight.shape[3]
    kv_local = key_value_weight.shape[1]
    q_cols = q_weight.shape[1]
    q_local = q_cols // head_dim
    group = q_local // kv_local
    kv_cols = kv_local * 2 * head_dim
    kv_flat = key_value_weight.reshape(key_value_weight.shape[0], kv_cols)
    own_first = lax.axis_index(("ctx", "wt")) * tok_rows
    own_ids = own_first + jnp.arange(tok_rows, dtype=jnp.int32)
    own_positions = token_positions(own_ids, block_order, block_len)
    widened = tokens.astype(jnp.float32)
    normalized_input = (
        widened * lax.rsqrt(jnp.mean(widened * widened, axis=1, keepdims=True) + epsilon)
    ).astype(jnp.bfloat16)
    queries = jnp.dot(
        normalized_input,
        lax.all_gather(q_weight, "wt", axis=0, tiled=True),
        preferred_element_type=jnp.float32,
    )
    key_value_rows = jnp.dot(
        normalized_input,
        lax.all_gather(kv_flat, "wt", axis=0, tiled=True),
        preferred_element_type=jnp.float32,
    )
    queries = queries.reshape(tok_rows, q_local, head_dim)
    key_value_rows = key_value_rows.reshape(tok_rows, kv_local, 2, head_dim)
    q_rot = rotary(queries, own_positions, head_dim).astype(jnp.bfloat16)
    k_rot = rotary(key_value_rows[:, :, 0, :], own_positions, head_dim).astype(jnp.bfloat16)
    value_rows = key_value_rows[:, :, 1, :].astype(jnp.bfloat16)
    q_grouped = jnp.transpose(q_rot.reshape(tok_rows, kv_local, group, head_dim), (1, 2, 0, 3))
    q_grouped = q_grouped.reshape(kv_local, group * tok_rows, head_dim)
    query_positions = jnp.tile(own_positions, group)
    score_factor = 1.0 / head_dim**0.5
    key_part = lax.all_gather(k_rot, ("ctx", "wt"), axis=0, tiled=True)
    value_part = lax.all_gather(value_rows, ("ctx", "wt"), axis=0, tiled=True)
    count = key_part.shape[0]
    key_ids = jnp.arange(count, dtype=jnp.int32)
    key_positions = token_positions(key_ids, block_order, block_len)
    visible = query_positions[:, None] >= key_positions[None, :]
    old_max = jnp.full((kv_local, group * tok_rows), -1e30, jnp.float32)
    scores = (
        jnp.einsum("hqd,khd->hqk", q_grouped, key_part, preferred_element_type=jnp.float32)
        * score_factor
    )
    scores = jnp.where(visible[None], scores, -1e30)
    new_max = jnp.maximum(old_max, jnp.max(scores, axis=2))
    weights = jnp.where(visible[None], jnp.exp(scores - new_max[..., None]), 0.0)
    new_total = jnp.sum(weights, axis=2)
    new_acc = jnp.einsum(
        "hqk,khd->hqd", weights.astype(jnp.bfloat16), value_part, preferred_element_type=jnp.float32
    )
    heads_out = new_acc / new_total[..., None]
    heads_out = jnp.transpose(heads_out.reshape(kv_local, group, tok_rows, head_dim), (2, 0, 1, 3))
    heads_out = heads_out.reshape(tok_rows, q_cols).astype(jnp.bfloat16)
    partial_out = jnp.dot(
        heads_out,
        lax.all_gather(out_weight, "wt", axis=1, tiled=True),
        preferred_element_type=jnp.float32,
    )
    return lax.psum_scatter(
        partial_out.astype(jnp.bfloat16), "sub", scatter_dimension=1, tiled=True
    )


def solution(mesh):
    in_specs = (
        P(("parts", "ctx", "wt"), None),
        P("parts"),
        P("wt", "sub"),
        P("wt", "sub", None, None),
        P("sub", "wt"),
    )
    out_specs = P(("parts", "ctx", "wt"), "sub")
    return jax.shard_map(body, mesh=mesh, in_specs=in_specs, out_specs=out_specs, check_vma=False)
```

profile of v0, /device:TPU:0, one launch (start us, length us, event | category | flops | bytes accessed | tf_op | source)
XLA Modules:
  0.0 318.9 jit_solution(17308050258334250507)
XLA Ops:
  6.5 0.0 all-gather.7.cloned.1.call-start
  6.5 4.1 %reshape.158 = bf16[2048,512]{1,0:T(8,128)(2,1)} reshape(bf16[2048,2,2,128]{3,2,1,0:T(2,128)(2,1)} %param.8) | data formatting | bytes 4194304 | tf_op jit(solution)/shard_map/reshape | solution.py:37
  10.6 0.0 all-gather.7.cloned.1.call-update
  10.7 0.0 copy-start.1
  10.7 0.0 copy-start
  10.7 0.0 all-gather.5.cloned.1.call-start
  10.7 0.7 all-gather.5.cloned.1.call-update
  11.4 0.0 all-gather.9.cloned.1.call-start
  11.5 0.7 all-gather.9.cloned.1.call-update
  12.2 0.0 reduce-scatter.2.cloned.1.call-start
  12.3 0.0 copy-done.1
  12.3 0.1 select_reduce_fusion.1
  12.4 0.1 select_reduce_fusion
  12.5 0.3 multiply_cosine_fusion
  12.8 0.1 pad_maximum_fusion
  12.9 0.0 copy-done
  12.9 0.3 fusion.3
  13.2 0.4 broadcast_compare_fusion
  13.6 56.7 %all-gather.7.cloned.1.call-done = bf16[4096,512]{1,0:T(8,128)(2,1)} async-done(((bf16[2048,512]{1,0:T(8,128)(2,1)}), bf16[4096,512]{1,0:T(8,128)(2,1)}) %all-gather.7.cloned.1.call-update) | async-done | bytes 4194320 | tf_op jit(solution)/shard_map/all_gather | solution.py:52
  70.3 2.9 fusion.17
  73.2 0.2 reshape.159
  73.4 0.1 slice.27
  73.5 0.1 slice.30
  73.7 0.1 slice_negate_fusion.1
  73.8 0.1 fusion.23
  73.9 31.9 %all_gather.17 = bf16[1024,2,128]{2,0,1:T(8,128)(2,1)S(1)} all-gather(bf16[128,2,128]{2,0,1:T(8,128)(2,1)S(1)} %fusion.23), channel_id=1, replica_groups=mesh['parts'=2,'ctx'=4,'wt'=2,'sub'=2] {'ctx','wt'}, dimensions={0}, use_global_device_ids=true | all-gather | bytes 589824 | tf_op jit(solution)/shard_map/all_gather | solution.py:64
  105.8 31.8 %all-gather = bf16[1024,2,1,128]{3,0,1,2:T(8,128)(2,1)S(1)} all-gather(bf16[128,2,1,128]{3,0,1,2:T(8,128)(2,1)S(1)} %copy.24), channel_id=2, replica_groups=mesh['parts'=2,'ctx'=4,'wt'=2,'sub'=2] {'ctx','wt'}, dimensions={0}, use_global_device_ids=true | all-gather | bytes 589824 | tf_op jit(solution)/shard_map/all_gather | solution.py:65
  137.6 55.1 %all-gather.5.cloned.1.call-done = bf16[4096,1024]{1,0:T(8,128)(2,1)} async-done(((bf16[2048,1024]{1,0:T(8,128)(2,1)}), bf16[4096,1024]{1,0:T(8,128)(2,1)}) %all-gather.5.cloned.1.call-update) | async-done | bytes 8388624 | tf_op jit(solution)/shard_map/all_gather | solution.py:47
  192.7 4.7 %fusion.19 = f32[128,1024]{1,0:T(8,128)S(1)} fusion(bf16[4096,1024]{1,0:T(8,128)(2,1)} %all-gather.5.cloned.1.call-done, bf16[128,4096]{1,0:T(8,128)(2,1)S(1)} %copy-done, f32[128]{0:T(128)S(1)} %add_rsqrt_fusion), kind=kOutput, calls=%fused_computation.21 | convolution fusion | flops 1075314688 | bytes 9961984 | tf_op jit(solution)/shard_map/dot_general | solution.py:45
  197.4 0.2 reshape.155
  197.6 0.1 copy.19
  197.7 0.2 slice_negate_fusion
  197.9 0.4 fusion.21
  198.4 1.1 fusion
  199.5 1.5 fusion.1
  200.9 1.6 fusion.11
  202.5 0.2 copy.16
  202.7 95.2 %all-gather.9.cloned.1.call-done = bf16[1024,4096]{1,0:T(8,128)(2,1)} async-done(((bf16[1024,2048]{1,0:T(8,128)(2,1)}), bf16[1024,4096]{1,0:T(8,128)(2,1)}) %all-gather.9.cloned.1.call-update) | async-done | bytes 8388624 | tf_op jit(solution)/shard_map/all_gather | solution.py:87
  297.9 5.7 %convolution_convert_fusion = bf16[128,4096]{1,0:T(8,128)(2,1)} fusion(bf16[128,1024]{0,1:T(8,128)(2,1)S(1)} %bitcast.31, bf16[1024,4096]{1,0:T(8,128)(2,1)} %all-gather.9.cloned.1.call-done), kind=kOutput, calls=%fused_computation | convolution fusion | flops 1074266112 | bytes 9699328 | tf_op jit(solution)/shard_map/dot_general | solution.py:85
  303.7 0.0 reduce-scatter.2.cloned.1.call-update
  303.7 8.7 %reduce-scatter.2.cloned.1.call-done = bf16[128,2048]{1,0:T(8,128)(2,1)} async-done(((bf16[128,4096]{1,0:T(8,128)(2,1)}), bf16[128,2048]{1,0:T(8,128)(2,1)}) %reduce-scatter.2.cloned.1.call-update) | async-done | bytes 524304 | tf_op jit(solution)/shard_map/reduce_scatter | solution.py:90
  (11 shorter events, 0.1 us)
Async XLA Ops:
  6.5 63.7 %all-gather.7.cloned.1.call-start = ((), (), s32[]{:S(2)}) async-start(), calls=%async_computation.2 | async-start | bytes 6291456 | tf_op jit(solution)/shard_map/all_gather | solution.py:52
  10.7 1.6 copy-start.1
  10.7 2.2 copy-start
  10.7 182.0 %all-gather.5.cloned.1.call-start = ((), (), s32[]{:S(2)}) async-start(), calls=%async_computation.1 | async-start | bytes 12582912 | tf_op jit(solution)/shard_map/all_gather | solution.py:47
  11.4 286.5 %all-gather.9.cloned.1.call-start = ((), (), s32[]{:S(2)}) async-start(), calls=%async_computation.3 | async-start | bytes 12582912 | tf_op jit(solution)/shard_map/all_gather | solution.py:87
  12.2 300.2 %reduce-scatter.2.cloned.1.call-start = ((), (), s32[]{:S(2)}) async-start(), calls=%async_computation.4 | async-start | bytes 1572864 | tf_op jit(solution)/shard_map/reduce_scatter | solution.py:90
Sparse Core Ops, SparseCore 0:
  10.8 59.4 all-gather.6
  71.8 120.8 all-gather.4
  194.3 103.6 all-gather.8
  303.8 8.5 reduce-scatter.1
where the time goes:
time: 319 us
  waiting for transfers between devices  217 us (68%)
  blocking collectives  63.7 us (20%)
  matrix products  16 us (5%)
  between operations  13.3 us (4%)
  local copies, waits for them, and re-layouts  5.11 us (2%)
  other arithmetic  3.58 us (1%)
    all_gather x1, waiting for transfers between devices, body(): lax.all_gather(out_weight, 'wt', axis=1, tiled=True)  95.2 us
    all_gather x1, waiting for transfers between devices, body(): lax.all_gather(kv_flat, 'wt', axis=0, tiled=True)  56.7 us
    all_gather x1, waiting for transfers between devices, body(): lax.all_gather(q_weight, 'wt', axis=0, tiled=True)  55.1 us
    all_gather x1, blocking collectives, body(): key_part = lax.all_gather(k_rot, ('ctx', 'wt'), axis=0, tiled=True)  31.9 us
    all_gather x1, blocking collectives, body(): value_part = lax.all_gather(value_rows, ('ctx', 'wt'), axis=0, tiled=True)  31.8 us
    reduce_scatter x1, waiting for transfers between devices, body(): lax.psum_scatter(partial_out.astype(jnp.bfloat16), 'sub', scatter_dimensi...  8.72 us
  transfers between devices with their start and end apart: 4, of which 4 were waited for; matrix products, arithmetic and copies ran while one was open for 5% of the time, Pallas kernels for 0%

commit v1 on v0

--- a/solution.py
+++ b/solution.py
@@ -61,8 +61,13 @@
     q_grouped = q_grouped.reshape(kv_local, group * tok_rows, head_dim)
     query_positions = jnp.tile(own_positions, group)
     score_factor = 1.0 / head_dim**0.5
-    key_part = lax.all_gather(k_rot, ("ctx", "wt"), axis=0, tiled=True)
-    value_part = lax.all_gather(value_rows, ("ctx", "wt"), axis=0, tiled=True)
+    key_part, value_part = jnp.split(
+        lax.all_gather(
+            jnp.concatenate([k_rot, value_rows], axis=1), ("ctx", "wt"), axis=0, tiled=True
+        ),
+        [k_rot.shape[1]],
+        axis=1,
+    )
     count = key_part.shape[0]
     key_ids = jnp.arange(count, dtype=jnp.int32)
     key_positions = token_positions(key_ids, block_order, block_len)

time: 319 us -> 344 us (1.078)
  waiting for transfers between devices: 217 us -> 304 us
  blocking collectives: 63.7 us -> 0 us
    all_gather x2 -> x0, blocking collectives: 63.7 us -> none  [the longest x1 31.9 us: body(): key_part = lax.all_gather(k_rot, ('ctx', 'wt'), axis=0, tiled=True)]
    all_gather x1, waiting for transfers between devices: 55.1 us -> 100 us  [body(): lax.all_gather(q_weight, 'wt', axis=0, tiled=True)]
    all_gather x0 -> x1, waiting for transfers between devices: none -> 36.7 us  [body(): lax.all_gather(jnp.concatenate([k_rot, value_rows], axis=1), ('ctx', 'wt'...]
    all_gather x1, waiting for transfers between devices: 95.2 us -> 99.3 us  [body(): lax.all_gather(out_weight, 'wt', axis=1, tiled=True)]
  transfers between devices with their start and end apart: 4 -> 5, of which waited for: 4 -> 5; matrix products, arithmetic and copies ran while one was open for 5% -> 5% of each run, Pallas kernels for 0% -> 0%
where the time goes in v1:
time: 344 us; the launch traced here: 343 us
  waiting for transfers between devices  304 us (88%)
  matrix products  16.5 us (5%)
  between operations  13.3 us (4%)
  local copies, waits for them, and re-layouts  5.11 us (1%)
  other arithmetic  4.25 us (1%)
    all_gather x1, waiting for transfers between devices, body(): lax.all_gather(q_weight, 'wt', axis=0, tiled=True)  100 us
    all_gather x1, waiting for transfers between devices, body(): lax.all_gather(out_weight, 'wt', axis=1, tiled=True)  99.3 us
    all_gather x1, waiting for transfers between devices, body(): lax.all_gather(kv_flat, 'wt', axis=0, tiled=True)  57.9 us
    all_gather x1, waiting for transfers between devices, body(): lax.all_gather(jnp.concatenate([k_rot, value_rows], axis=1), ('ctx', 'wt'...  36.7 us
    reduce_scatter x1, waiting for transfers between devices, body(): lax.psum_scatter(partial_out.astype(jnp.bfloat16), 'sub', scatter_dimensi...  8.72 us
  transfers between devices with their start and end apart: 5, of which 5 were waited for; matrix products, arithmetic and copies ran while one was open for 5% of the time, Pallas kernels for 0%

profile of v1, /device:TPU:0, one launch (start us, length us, event | category | flops | bytes accessed | tf_op | source)
XLA Modules:
  0.0 343.4 jit_solution(928204523938229370)
XLA Ops:
  6.5 0.0 all-gather.7.cloned.1.call-start
  6.5 4.1 %reshape.158 = bf16[2048,512]{1,0:T(8,128)(2,1)} reshape(bf16[2048,2,2,128]{3,2,1,0:T(2,128)(2,1)} %param.8) | data formatting | bytes 4194304 | tf_op jit(solution)/shard_map/reshape | solution.py:37
  10.6 0.0 copy-start.1
  10.6 0.0 copy-start
  10.6 0.0 all-gather.7.cloned.1.call-update
  10.7 0.0 all-gather.5.cloned.1.call-start
  10.7 0.7 all-gather.5.cloned.1.call-update
  11.4 0.0 all-gather.9.cloned.1.call-start
  11.5 0.0 copy-done.1
  11.5 0.1 select_reduce_fusion.1
  11.6 0.3 multiply_cosine_fusion
  11.9 0.1 pad_maximum_fusion.1
  12.0 0.0 copy-done
  12.1 0.3 fusion.3
  12.4 57.9 %all-gather.7.cloned.1.call-done = bf16[4096,512]{1,0:T(8,128)(2,1)} async-done(((bf16[2048,512]{1,0:T(8,128)(2,1)}), bf16[4096,512]{1,0:T(8,128)(2,1)}) %all-gather.7.cloned.1.call-update) | async-done | bytes 4194320 | tf_op jit(solution)/shard_map/all_gather | solution.py:52
  70.3 2.9 fusion.19
  73.2 0.2 reshape.159
  73.4 0.1 slice.30
  73.5 0.1 slice.27
  73.7 0.1 slice_negate_fusion.1
  73.8 0.1 fusion.25
  73.9 0.7 pad_maximum_fusion
  74.6 0.0 all-gather.9.cloned.1.call-update
  74.6 0.0 all-gather.11.cloned.1.call-start
  74.7 0.5 all-gather.11.cloned.1.call-update
  75.2 0.0 reduce-scatter.2.cloned.1.call-start
  75.2 0.1 select_reduce_fusion
  75.4 0.4 broadcast_compare_fusion
  75.7 100.1 %all-gather.5.cloned.1.call-done = bf16[4096,1024]{1,0:T(8,128)(2,1)} async-done(((bf16[2048,1024]{1,0:T(8,128)(2,1)}), bf16[4096,1024]{1,0:T(8,128)(2,1)}) %all-gather.5.cloned.1.call-update) | async-done | bytes 8388624 | tf_op jit(solution)/shard_map/all_gather | solution.py:47
  175.9 4.7 %fusion.21 = f32[128,1024]{1,0:T(8,128)S(1)} fusion(bf16[4096,1024]{1,0:T(8,128)(2,1)} %all-gather.5.cloned.1.call-done, bf16[128,4096]{1,0:T(8,128)(2,1)S(1)} %copy-done, f32[128]{0:T(128)S(1)} %add_rsqrt_fusion), kind=kOutput, calls=%fused_computation.23 | convolution fusion | flops 1075314688 | bytes 9961984 | tf_op jit(solution)/shard_map/dot_general | solution.py:45
  180.5 0.2 reshape.155
  180.8 0.1 copy.19
  180.9 0.2 slice_negate_fusion
  181.1 0.4 fusion.23
  181.6 36.7 %all-gather.9.cloned.1.call-done = bf16[1024,4,128]{2,0,1:T(8,128)(2,1)} async-done(((bf16[128,4,128]{2,0,1:T(8,128)(2,1)}), bf16[1024,4,128]{2,0,1:T(8,128)(2,1)}) %all-gather.9.cloned.1.call-update) | async-done | bytes 1048592 | tf_op jit(solution)/shard_map/all_gather | solution.py:65
  218.3 0.0 copy-start.2
  218.3 2.2 fusion
  220.5 1.5 fusion.1
  221.9 0.0 copy-done.2
  221.9 1.1 fusion.11
  223.0 0.2 copy.16
  223.2 99.3 %all-gather.11.cloned.1.call-done = bf16[1024,4096]{1,0:T(8,128)(2,1)} async-done(((bf16[1024,2048]{1,0:T(8,128)(2,1)}), bf16[1024,4096]{1,0:T(8,128)(2,1)}) %all-gather.11.cloned.1.call-update) | async-done | bytes 8388624 | tf_op jit(solution)/shard_map/all_gather | solution.py:92
  322.5 5.6 %convolution_convert_fusion = bf16[128,4096]{1,0:T(8,128)(2,1)} fusion(bf16[128,1024]{0,1:T(8,128)(2,1)S(1)} %bitcast.30, bf16[1024,4096]{1,0:T(8,128)(2,1)} %all-gather.11.cloned.1.call-done), kind=kOutput, calls=%fused_computation | convolution fusion | flops 1074266112 | bytes 9699328 | tf_op jit(solution)/shard_map/dot_general | solution.py:90
  328.1 0.0 reduce-scatter.2.cloned.1.call-update
  328.1 8.7 %reduce-scatter.2.cloned.1.call-done = bf16[128,2048]{1,0:T(8,128)(2,1)} async-done(((bf16[128,4096]{1,0:T(8,128)(2,1)}), bf16[128,2048]{1,0:T(8,128)(2,1)}) %reduce-scatter.2.cloned.1.call-update) | async-done | bytes 524304 | tf_op jit(solution)/shard_map/reduce_scatter | solution.py:95
  (11 shorter events, 0.1 us)
Async XLA Ops:
  6.5 63.7 %all-gather.7.cloned.1.call-start = ((), (), s32[]{:S(2)}) async-start(), calls=%async_computation.2 | async-start | bytes 6291456 | tf_op jit(solution)/shard_map/all_gather | solution.py:52
  10.6 0.9 copy-start.1
  10.6 1.4 copy-start
  10.7 165.2 %all-gather.5.cloned.1.call-start = ((), (), s32[]{:S(2)}) async-start(), calls=%async_computation.1 | async-start | bytes 12582912 | tf_op jit(solution)/shard_map/all_gather | solution.py:47
  11.4 206.9 %all-gather.9.cloned.1.call-start = ((), (), s32[]{:S(2)}) async-start(), calls=%async_computation.3 | async-start | bytes 1179648 | tf_op jit(solution)/shard_map/all_gather | solution.py:65
  74.6 247.9 %all-gather.11.cloned.1.call-start = ((), (), s32[]{:S(2)}) async-start(), calls=%async_computation.4 | async-start | bytes 12582912 | tf_op jit(solution)/shard_map/all_gather | solution.py:92
  75.2 261.7 %reduce-scatter.2.cloned.1.call-start = ((), (), s32[]{:S(2)}) async-start(), calls=%async_computation.5 | async-start | bytes 1572864 | tf_op jit(solution)/shard_map/reduce_scatter | solution.py:95
  218.3 3.7 %copy-start.2 = (bf16[1024,4,128]{2,0,1:T(8,128)(2,1)S(1)}, bf16[1024,4,128]{2,0,1:T(8,128)(2,1)}, u32[]{:S(2)}) copy-start(bf16[1024,4,128]{2,0,1:T(8,128)(2,1)} %all-gather.9.cloned.1.call-done) | copy-start | bytes 3145732
Sparse Core Ops, SparseCore 0:
  10.8 59.4 all-gather.6
  71.8 103.9 all-gather.4
  178.0 40.1 all-gather.8
  219.7 102.7 all-gather.10
  328.2 8.5 reduce-scatter.1
